TPU v7x, 512 devices: a whole 4x8x8 slice. The times are simulated.
512 devices in a mesh: head: 8 (over y), ctx: 64 (over x, z, core).
Axes of the slice: x: 4, y: 8, z: 8, core: 2. Of those that a mesh axis runs over, the one named last changes fastest.
Arguments:
- queries: bfloat16 [32768, 1024], P('ctx', 'head'), may hold values from -40 to 40
- keys: bfloat16 [32768, 128], P('ctx'), may hold values from -5 to 5
- values: bfloat16 [32768, 128], P('ctx'), may hold values from -6 to 6
- d_out: bfloat16 [64, 512, 1024], P('ctx', 'head'), may hold values from -6 to 6
- lengths: int32 [64], replicated, may hold values from 1 to 1024, 32768 in all
Outputs:
- grad_queries: bfloat16 [32768, 1024], P('ctx', 'head')
- grad_keys: bfloat16 [64, 512, 128], P('ctx', 'head')
- grad_values: bfloat16 [64, 512, 128], P('ctx', 'head')
Inputs may be any that keep to these rules, and one draw needn't show every extreme that they name: `lengths`: 64 documents that fill the 32768 tokens exactly; the longest has exactly 1024 tokens.
All inputs are finite; a program needn't handle non-finite values.
Results may differ from a plain program's by a relative error of at most 0.0055.
Values may be sent and summed in bfloat16 or wider, within the bound.
No kernel may reach another device: no remote copies, remote signals or barrier semaphores. Data moves between devices by JAX's collectives and lax.ppermute only.
A program may use at most 64 MiB of HBM per device.

v0:
```python
from functools import reduce

import jax
import jax.numpy as jnp
from jax import lax
from jax.sharding import PartitionSpec as P

DH = 128
SPAN = 2


def from_behind(value, axis, steps):
    count = lax.axis_size(axis)
    leading, last = (max(0, -steps), min(count, count - steps))
    return lax.ppermute(value, axis, [(source, source + steps) for source in range(leading, last)])


def shards(queries, keys, values, d_out, lengths):
    rows = keys.shape[0]
    heads = queries.shape[1] // DH
    scale = DH ** (-0.5)
    regrouped = lax.all_to_all(d_out, "head", split_axis=2, concat_axis=1, tiled=True)
    grad_rows = regrouped.reshape(rows, heads, DH)
    query_rows = queries.reshape(rows, heads, DH)
    shard = lax.axis_index("ctx")
    offsets = jnp.arange(rows, dtype=jnp.int32)
    query_pos = shard * rows + offsets
    starts = jnp.cumsum(lengths) - lengths
    query_start = jnp.max(
        jnp.where(starts[None, :] <= query_pos[:, None], starts[None, :], 0), axis=1
    )
    windows = [(keys, values)]
    for distance in range(1, SPAN + 1):
        windows.append(from_behind((keys, values), "ctx", distance))
    score_tiles = []
    for distance in range(SPAN + 1):
        key_pos = (shard - distance) * rows + offsets
        visible = (key_pos[None, :] <= query_pos[:, None]) & (
            key_pos[None, :] >= query_start[:, None]
        )
        plain = (
            jnp.einsum(
                "thd,kd->htk", query_rows, windows[distance][0], preferred_element_type=jnp.float32
            )
            * scale
        )
        score_tiles.append(jnp.where(visible[None], plain, -1e30))
    highest = reduce(jnp.maximum, [jnp.max(tile, axis=2) for tile in score_tiles])
    total = reduce(
        jnp.add, [jnp.sum(jnp.exp(tile - highest[:, :, None]), axis=2) for tile in score_tiles]
    )
    log_total = highest + jnp.log(total)
    prob_tiles = [jnp.exp(tile - log_total[:, :, None]) for tile in score_tiles]
    weight_tiles = [tile.astype(jnp.bfloat16) for tile in prob_tiles]
    attended = reduce(
        jnp.add,
        [
            jnp.einsum(
                "htk,kd->thd", weight_tiles[i], windows[i][1], preferred_element_type=jnp.float32
            )
            for i in range(SPAN + 1)
        ],
    )
    delta = jnp.sum(grad_rows.astype(jnp.float32) * attended, axis=2)
    delta_rows = delta.T[:, :, None]
    query_grad = jnp.zeros((rows, heads, DH), jnp.float32)
    key_terms = []
    for distance in range(SPAN + 1):
        dprobs = jnp.einsum(
            "thd,kd->htk", grad_rows, windows[distance][1], preferred_element_type=jnp.float32
        )
        dscores = (prob_tiles[distance] * (dprobs - delta_rows)).astype(jnp.bfloat16)
        query_grad = query_grad + jnp.einsum(
            "htk,kd->thd", dscores, windows[distance][0], preferred_element_type=jnp.float32
        )
        key_term = (
            jnp.einsum("htk,thd->kd", dscores, query_rows, preferred_element_type=jnp.float32)
            * scale
        )
        value_term = jnp.einsum(
            "htk,thd->kd", weight_tiles[distance], grad_rows, preferred_element_type=jnp.float32
        )
        key_terms.append((key_term, value_term))
    grad_queries = (query_grad * scale).astype(jnp.bfloat16).reshape(rows, heads * DH)
    key_total = key_terms[0][0]
    value_total = key_terms[0][1]
    for distance in range(1, SPAN + 1):
        returned = from_behind(key_terms[distance], "ctx", -distance)
        key_total = key_total + returned[0]
        value_total = value_total + returned[1]
    key_share, value_share = (
        lax.psum_scatter(key_total[None], "head", scatter_dimension=1, tiled=True),
        lax.psum_scatter(value_total[None], "head", scatter_dimension=1, tiled=True),
    )
    return (grad_queries, key_share.astype(jnp.bfloat16), value_share.astype(jnp.bfloat16))


def solution(mesh):
    in_specs = (P("ctx", "head"), P("ctx", None), P("ctx", None), P("ctx", "head", None), P())
    out_specs = (P("ctx", "head"), P("ctx", "head", None), P("ctx", "head", None))
    return jax.shard_map(shards, mesh=mesh, in_specs=in_specs, out_specs=out_specs, check_vma=False)
```

profile of v0, /device:TPU:6, one launch (start us, length us, event | category | flops | bytes accessed | tf_op | source)
XLA Modules:
  0.0 151.4 jit_solution(13574826883915865106)
XLA Ops:
  7.2 2.1 %collective-permute-start = (bf16[512,128]{1,0:T(8,128)(2,1)}, bf16[512,128]{1,0:T(8,128)(2,1)S(1)}, u32[]{:S(2)}, u32[]{:S(2)}) collective-permute-start(bf16[512,128]{1,0:T(8,128)(2,1)} %param.6), channel_id=1, source_target_pairs={{0,1},{1,2},{2,3},{3,4},{4,5},{5,6},{6,7},{7,8},{8,9},{9,10},{10,1... | collective-permute-start | bytes 393224 | tf_op jit(solution)/shard_map/ppermute | solution.py:15
  9.2 4.3 %collective-permute-start.1 = (bf16[512,128]{1,0:T(8,128)(2,1)}, bf16[512,128]{1,0:T(8,128)(2,1)S(1)}, u32[]{:S(2)}, u32[]{:S(2)}) collective-permute-start(bf16[512,128]{1,0:T(8,128)(2,1)} %param.6), channel_id=1, source_target_pairs={{0,2},{1,3},{2,4},{3,5},{4,6},{5,7},{6,8},{7,9},{8,10},{9,11},{10,... | collective-permute-start | bytes 393224 | tf_op jit(solution)/shard_map/ppermute | solution.py:15
  13.5 4.1 %collective-permute-start.2 = (bf16[512,128]{1,0:T(8,128)(2,1)}, bf16[512,128]{1,0:T(8,128)(2,1)S(1)}, u32[]{:S(2)}, u32[]{:S(2)}) collective-permute-start(bf16[512,128]{1,0:T(8,128)(2,1)} %param.7), channel_id=1, source_target_pairs={{0,1},{1,2},{2,3},{3,4},{4,5},{5,6},{6,7},{7,8},{8,9},{9,10},{10,1... | collective-permute-start | bytes 393224 | tf_op jit(solution)/shard_map/ppermute | solution.py:15
  17.6 4.3 %collective-permute-start.3 = (bf16[512,128]{1,0:T(8,128)(2,1)}, bf16[512,128]{1,0:T(8,128)(2,1)}, u32[]{:S(2)}, u32[]{:S(2)}) collective-permute-start(bf16[512,128]{1,0:T(8,128)(2,1)} %param.7), channel_id=1, source_target_pairs={{0,2},{1,3},{2,4},{3,5},{4,6},{5,7},{6,8},{7,9},{8,10},{9,11},{10,... | collective-permute-start | bytes 393224 | tf_op jit(solution)/shard_map/ppermute | solution.py:15
  21.9 1.2 copy.23
  23.7 2.3 %reduce.8 = bf16[1024,64]{1,0:T(8,128)(2,1)S(1)} reduce(bf16[1024,1,64]{2,1,0:T(2,128)(2,1)S(1)} %bitcast.164, bf16[]{:T(256)} %broadcast.278), dimensions={1}, to_apply=%bitcast.124.reduce_sub_computation | reduce | bytes 262146
  25.9 0.9 reshape.476
  26.8 7.2 %all-to-all-start = ((bf16[8,2,4096]{2,1,0:T(2,128)(2,1)}), bf16[8,2,4096]{2,1,0:T(2,128)(2,1)}, u32[]{:S(2)}, u32[]{:S(2)}) async-start(bf16[8,2,4096]{2,1,0:T(2,128)(2,1)} %reshape.476), calls=%async_computation | async-start | bytes 262144 | tf_op jit(solution)/shard_map/all_to_all | solution.py:22
  38.0 1.0 convolution_add_fusion.4
  39.0 4.4 %all-to-all-done = bf16[8,2,4096]{2,1,0:T(2,128)(2,1)} async-done(((bf16[8,2,4096]{2,1,0:T(2,128)(2,1)}), bf16[8,2,4096]{2,1,0:T(2,128)(2,1)}, u32[]{:S(2)}, u32[]{:S(2)}) %all-to-all-start) | async-done | bytes 131104 | tf_op jit(solution)/shard_map/all_to_all | solution.py:22
  43.4 1.8 %reshape.477 = bf16[1024,1,64]{2,1,0:T(2,128)(2,1)} reshape(bf16[8,2,4096]{2,1,0:T(2,128)(2,1)} %all-to-all-done) | data formatting | bytes 262144
  45.3 1.2 copy.24
  46.6 1.0 fusion.40
  47.6 2.0 %collective-permute-start.6 = (f32[512,128]{1,0:T(8,128)}, f32[512,128]{1,0:T(8,128)}, u32[]{:S(2)}, u32[]{:S(2)}) collective-permute-start(f32[512,128]{1,0:T(8,128)} %fusion.40), channel_id=1, source_target_pairs={{1,0},{2,1},{3,2},{4,3},{5,4},{6,5},{7,6},{8,7},{9,8},{10,9},{11,1... | collective-permute-start | bytes 786440 | tf_op jit(solution)/shard_map/ppermute | solution.py:15
  49.6 1.0 fusion.43
  50.6 4.2 %collective-permute-start.7 = (f32[512,128]{1,0:T(8,128)}, f32[512,128]{1,0:T(8,128)}, u32[]{:S(2)}, u32[]{:S(2)}) collective-permute-start(f32[512,128]{1,0:T(8,128)} %fusion.43), channel_id=1, source_target_pairs={{2,0},{3,1},{4,2},{5,3},{6,4},{7,5},{8,6},{9,7},{10,8},{11,9},{12,... | collective-permute-start | bytes 786440 | tf_op jit(solution)/shard_map/ppermute | solution.py:15
  54.8 0.7 copy.26
  55.6 1.8 %copy.27 = f32[512,1,128]{0,2,1:T(8,128)} copy(f32[512,1,128]{2,0,1:T(8,128)} %bitcast.165) | data formatting | bytes 524288 | tf_op jit(solution)/shard_map/convert_element_type | solution.py:64
  57.4 1.4 fusion.30
  58.8 1.2 fusion.20
  60.0 1.0 convolution_multiply_fusion.3
  61.0 4.0 %collective-permute-start.5 = (f32[512,128]{1,0:T(8,128)}, f32[512,128]{1,0:T(8,128)}, u32[]{:S(2)}, u32[]{:S(2)}) collective-permute-start(f32[512,128]{1,0:T(8,128)} %convolution_multiply_fusion.3), channel_id=1, source_target_pairs={{2,0},{3,1},{4,2},{5,3},{6,4},{7,5},{8,6},{9,7},{10,8},{11,9},{12,... | collective-permute-start | bytes 786440 | tf_op jit(solution)/shard_map/ppermute | solution.py:15
  65.4 2.1 %fusion.26 = f32[1,512,128]{2,1,0:T(8,128)} fusion(f32[512,128]{1,0:T(8,128)} %collective-permute-done.7, f32[512,128]{1,0:T(8,128)} %collective-permute-done.6, bf16[512,128]{1,0:T(8,128)(2,1)S(1)} %bitcast.161, f32[1,512,512]{1,2,0:T(8,128)S(1)} %get-tuple-element.11, f32[512]{0:T(512)S(1)} %log_add_fusion), kind=kOutput, calls=%fused_computation.40 | convolution fusion | flops 67764224 | bytes 1968128 | tf_op jit(solution)/shard_map/htk,thd->kd/dot_general | solution.py:80
  67.9 3.5 %collective-permute-start.4 = (f32[512,128]{1,0:T(8,128)S(1)}, f32[512,128]{1,0:T(8,128)S(1)}, u32[]{:S(2)}, u32[]{:S(2)}) collective-permute-start(f32[512,128]{1,0:T(8,128)S(1)} %convolution_multiply_fusion.4), channel_id=1, source_target_pairs={{1,0},{2,1},{3,2},{4,3},{5,4},{6,5},{7,6},{8,7},{9,8},{10,9},{11,1... | collective-permute-start | bytes 786440 | tf_op jit(solution)/shard_map/ppermute | solution.py:15
  71.7 3.5 %collective-permute-done.4 = f32[512,128]{1,0:T(8,128)S(1)} collective-permute-done((f32[512,128]{1,0:T(8,128)S(1)}, f32[512,128]{1,0:T(8,128)S(1)}, u32[]{:S(2)}, u32[]{:S(2)}) %collective-permute-start.4) | collective-permute-done | bytes 262176 | tf_op jit(solution)/shard_map/ppermute | solution.py:15
  75.2 2.0 %fusion.28 = f32[1,512,128]{2,1,0:T(8,128)} fusion(f32[512,128]{1,0:T(8,128)} %collective-permute-done.5, f32[512,128]{1,0:T(8,128)S(1)} %collective-permute-done.4, bf16[512,512]{0,1:T(8,128)(2,1)S(1)} %fusion.18, bf16[512,128]{1,0:T(8,128)(2,1)S(1)} %copy-done), kind=kOutput, calls=%fused_computation.42 | convolution fusion | flops 67305472 | bytes 1441792 | tf_op jit(solution)/shard_map/htk,thd->kd/dot_general | solution.py:77
  77.2 0.9 copy-done.7
  80.0 1.0 fusion.29
  81.1 21.0 %reduce-scatter.5.cloned.1.call-done = f32[1,64,128]{2,1,0:T(8,128)} async-done(((f32[1,512,128]{2,1,0:T(8,128)}), f32[1,64,128]{2,1,0:T(8,128)}) %reduce-scatter.5.cloned.1.call-update) | async-done | bytes 32784 | tf_op jit(solution)/shard_map/reduce_scatter | solution.py:93
  102.0 1.4 convert_element_type.52
  103.4 39.8 %reduce-scatter.3.cloned.1.call-done = f32[1,64,128]{2,1,0:T(8,128)} async-done(((f32[1,512,128]{2,1,0:T(8,128)}), f32[1,64,128]{2,1,0:T(8,128)}) %reduce-scatter.3.cloned.1.call-update) | async-done | bytes 32784 | tf_op jit(solution)/shard_map/reduce_scatter | solution.py:92
  143.2 1.4 convert_element_type.51
  (60 shorter events, 7.3 us)
Async XLA Ops:
  7.2 27.4 %copy-start = (bf16[512,128]{1,0:T(8,128)(2,1)S(1)}, bf16[512,128]{1,0:T(8,128)(2,1)}, u32[]{:S(2)}) copy-start(bf16[512,128]{1,0:T(8,128)(2,1)} %param.5) | copy-start | bytes 393220
  7.2 28.2 %collective-permute-start = (bf16[512,128]{1,0:T(8,128)(2,1)}, bf16[512,128]{1,0:T(8,128)(2,1)S(1)}, u32[]{:S(2)}, u32[]{:S(2)}) collective-permute-start(bf16[512,128]{1,0:T(8,128)(2,1)} %param.6), channel_id=1, source_target_pairs={{0,1},{1,2},{2,3},{3,4},{4,5},{5,6},{6,7},{7,8},{8,9},{9,10},{10,1... | collective-permute-start | bytes 393224 | tf_op jit(solution)/shard_map/ppermute | solution.py:15
  9.2 26.8 %collective-permute-start.1 = (bf16[512,128]{1,0:T(8,128)(2,1)}, bf16[512,128]{1,0:T(8,128)(2,1)S(1)}, u32[]{:S(2)}, u32[]{:S(2)}) collective-permute-start(bf16[512,128]{1,0:T(8,128)(2,1)} %param.6), channel_id=1, source_target_pairs={{0,2},{1,3},{2,4},{3,5},{4,6},{5,7},{6,8},{7,9},{8,10},{9,11},{10,... | collective-permute-start | bytes 393224 | tf_op jit(solution)/shard_map/ppermute | solution.py:15
  13.5 24.4 %collective-permute-start.2 = (bf16[512,128]{1,0:T(8,128)(2,1)}, bf16[512,128]{1,0:T(8,128)(2,1)S(1)}, u32[]{:S(2)}, u32[]{:S(2)}) collective-permute-start(bf16[512,128]{1,0:T(8,128)(2,1)} %param.7), channel_id=1, source_target_pairs={{0,1},{1,2},{2,3},{3,4},{4,5},{5,6},{6,7},{7,8},{8,9},{9,10},{10,1... | collective-permute-start | bytes 393224 | tf_op jit(solution)/shard_map/ppermute | solution.py:15
  17.6 39.7 %collective-permute-start.3 = (bf16[512,128]{1,0:T(8,128)(2,1)}, bf16[512,128]{1,0:T(8,128)(2,1)}, u32[]{:S(2)}, u32[]{:S(2)}) collective-permute-start(bf16[512,128]{1,0:T(8,128)(2,1)} %param.7), channel_id=1, source_target_pairs={{0,2},{1,3},{2,4},{3,5},{4,6},{5,7},{6,8},{7,9},{8,10},{9,11},{10,... | collective-permute-start | bytes 393224 | tf_op jit(solution)/shard_map/ppermute | solution.py:15
  26.8 7.3 %copy-start.12 = (s32[64]{0:T(128)S(1)}, s32[64]{0:T(128)}, u32[]{:S(2)}) copy-start(s32[64]{0:T(128)} %param.9) | copy-start | bytes 772
  26.8 16.6 %all-to-all-start = ((bf16[8,2,4096]{2,1,0:T(2,128)(2,1)}), bf16[8,2,4096]{2,1,0:T(2,128)(2,1)}, u32[]{:S(2)}, u32[]{:S(2)}) async-start(bf16[8,2,4096]{2,1,0:T(2,128)(2,1)} %reshape.476), calls=%async_computation | async-start | bytes 262144 | tf_op jit(solution)/shard_map/all_to_all | solution.py:22
  34.1 0.9 copy-start.6
  34.1 67.9 %reduce-scatter.5.cloned.1.call-start = ((), (), s32[]{:S(2)}) async-start(), calls=%async_computation.4 | async-start | bytes 294912 | tf_op jit(solution)/shard_map/reduce_scatter | solution.py:93
  35.4 0.6 copy-start.8
  36.0 0.7 copy-start.10
  36.7 0.9 copy-start.3
  37.9 1.0 copy-start.4
  47.6 17.8 %collective-permute-start.6 = (f32[512,128]{1,0:T(8,128)}, f32[512,128]{1,0:T(8,128)}, u32[]{:S(2)}, u32[]{:S(2)}) collective-permute-start(f32[512,128]{1,0:T(8,128)} %fusion.40), channel_id=1, source_target_pairs={{1,0},{2,1},{3,2},{4,3},{5,4},{6,5},{7,6},{8,7},{9,8},{10,9},{11,1... | collective-permute-start | bytes 786440 | tf_op jit(solution)/shard_map/ppermute | solution.py:15
  50.6 14.8 %collective-permute-start.7 = (f32[512,128]{1,0:T(8,128)}, f32[512,128]{1,0:T(8,128)}, u32[]{:S(2)}, u32[]{:S(2)}) collective-permute-start(f32[512,128]{1,0:T(8,128)} %fusion.43), channel_id=1, source_target_pairs={{2,0},{3,1},{4,2},{5,3},{6,4},{7,5},{8,6},{9,7},{10,8},{11,9},{12,... | collective-permute-start | bytes 786440 | tf_op jit(solution)/shard_map/ppermute | solution.py:15
  60.0 5.4 %copy-start.1 = (bf16[512,512]{0,1:T(8,128)(2,1)}, bf16[512,512]{0,1:T(8,128)(2,1)S(1)}, u32[]{:S(2)}) copy-start(bf16[512,512]{0,1:T(8,128)(2,1)S(1)} %fusion.20) | copy-start | bytes 1572868
  60.0 5.1 %copy-start.5 = (bf16[512,128]{1,0:T(8,128)(2,1)S(1)}, bf16[512,128]{1,0:T(8,128)(2,1)}, u32[]{:S(2)}) copy-start(bf16[512,128]{1,0:T(8,128)(2,1)} %copy-done.4) | copy-start | bytes 393220
  61.0 10.6 %collective-permute-start.5 = (f32[512,128]{1,0:T(8,128)}, f32[512,128]{1,0:T(8,128)}, u32[]{:S(2)}, u32[]{:S(2)}) collective-permute-start(f32[512,128]{1,0:T(8,128)} %convolution_multiply_fusion.3), channel_id=1, source_target_pairs={{2,0},{3,1},{4,2},{5,3},{6,4},{7,5},{8,6},{9,7},{10,8},{11,9},{12,... | collective-permute-start | bytes 786440 | tf_op jit(solution)/shard_map/ppermute | solution.py:15
  67.5 75.6 %reduce-scatter.3.cloned.1.call-start = ((), (), s32[]{:S(2)}) async-start(), calls=%async_computation.3 | async-start | bytes 294912 | tf_op jit(solution)/shard_map/reduce_scatter | solution.py:92
  67.9 7.3 %collective-permute-start.4 = (f32[512,128]{1,0:T(8,128)S(1)}, f32[512,128]{1,0:T(8,128)S(1)}, u32[]{:S(2)}, u32[]{:S(2)}) collective-permute-start(f32[512,128]{1,0:T(8,128)S(1)} %convolution_multiply_fusion.4), channel_id=1, source_target_pairs={{1,0},{2,1},{3,2},{4,3},{5,4},{6,5},{7,6},{8,7},{9,8},{10,9},{11,1... | collective-permute-start | bytes 786440 | tf_op jit(solution)/shard_map/ppermute | solution.py:15
  77.2 0.9 copy-start.7
  78.1 0.9 copy-start.9
  79.0 1.0 copy-start.2
  79.0 1.1 copy-start.11
Sparse Core Ops, SparseCore 0:
  67.6 34.3 reduce-scatter.4
  105.0 38.1 reduce-scatter.2
where the time goes:
time: 152 us; the launch traced here: 151 us
  waiting for transfers between devices  68.8 us (45%)
  starting transfers between devices  35.7 us (23%)
  matrix products  14.8 us (10%)
  between operations  14.4 us (9%)
  local copies, waits for them, and re-layouts  11.9 us (8%)
  other arithmetic  5.8 us (4%)
    reduce_scatter x1, waiting for transfers between devices, shards(): lax.psum_scatter(key_total[None], 'head', scatter_dimension=1, tiled=True)  39.8 us
    ppermute x8, starting transfers between devices, from_behind(): lax.ppermute(value, axis, [(source, source + steps) for source in range(l...  28.4 us
    reduce_scatter x1, waiting for transfers between devices, shards(): lax.psum_scatter(value_total[None], 'head', scatter_dimension=1, tiled=True)  21 us
    unnamed x31, local copies, waits for them, and re-layouts  8.03 us
    all_to_all x1, starting transfers between devices, shards(): lax.all_to_all(d_out, 'head', split_axis=2, concat_axis=1, tiled=True)  7.23 us
    all_to_all x1, waiting for transfers between devices, shards(): lax.all_to_all(d_out, 'head', split_axis=2, concat_axis=1, tiled=True)  4.45 us
    dot_general x3, matrix products, shards(): jnp.einsum('htk,thd->kd', weight_tiles[distance], grad_rows, preferred_el...  4.12 us
    ppermute x8, waiting for transfers between devices, from_behind(): lax.ppermute(value, axis, [(source, source + steps) for source in range(l...  3.57 us
  transfers between devices with their start and end apart: 11, of which 4 were waited for; matrix products, arithmetic and copies ran while one was open for 18% of the time, Pallas kernels for 0%

commit v1 on v0

v1 whole, which is shorter than its diff:
```python
import functools

import jax
import jax.numpy as jnp
from jax import lax
from jax.experimental import pallas as pl
from jax.experimental.pallas import tpu as pltpu
from jax.sharding import PartitionSpec as P

DH = 128
SPAN = 2
LOG2E = 1.4426950408889634


def shifted(value, axis, steps):
    count = lax.axis_size(axis)
    leading, last = (max(0, -steps), min(count, count - steps))
    return lax.ppermute(value, axis, [(source, source + steps) for source in range(leading, last)])


def nt(a, b):
    return lax.dot_general(a, b, (((1,), (1,)), ((), ())), preferred_element_type=jnp.float32)


def nn(a, b):
    return lax.dot_general(a, b, (((1,), (0,)), ((), ())), preferred_element_type=jnp.float32)


def attention_kernel(shard_ref, len_row_ref, len_col_ref, q_ref, do_ref, kv0_ref, kv1_ref, kv2_ref,
                     dq_ref, own_ref, one_ref, two_ref):
    rows = q_ref.shape[0]
    scale = DH ** (-0.5)
    first = shard_ref[0] * rows
    docs = len_row_ref.shape[1]
    j = lax.broadcasted_iota(jnp.int32, (docs, docs), 0)
    k = lax.broadcasted_iota(jnp.int32, (docs, docs), 1)
    ends = jnp.sum(jnp.where(k <= j, len_row_ref[...], 0), axis=1, keepdims=True)
    query_pos = first + lax.broadcasted_iota(jnp.int32, (1, rows), 1)
    start = jnp.sum(jnp.where(ends <= query_pos, len_col_ref[...], 0), axis=0, keepdims=True)
    q = q_ref[...]
    do = do_ref[...]
    sub = lax.broadcasted_iota(jnp.int32, (rows, rows), 0)
    lane = lax.broadcasted_iota(jnp.int32, (rows, rows), 1)
    kvs = (kv0_ref, kv1_ref, kv2_ref)
    scores = []
    for distance in range(SPAN + 1):
        plain = nt(kvs[distance][:rows], q) * (scale * LOG2E)
        seen = sub >= start - (first - distance * rows)
        if distance == 0:
            seen = seen & (sub <= lane)
        scores.append(jnp.where(seen, plain, -1e30))
    highest = functools.reduce(jnp.maximum, [jnp.max(s, axis=0, keepdims=True) for s in scores])
    probs = [jnp.exp2(s - highest) for s in scores]
    total = functools.reduce(jnp.add, [jnp.sum(p, axis=0, keepdims=True) for p in probs])
    inverse = 1.0 / total
    probs = [p * inverse for p in probs]
    weights = [p.astype(jnp.bfloat16) for p in probs]
    dprobs = [nt(kv[rows:], do) for kv in kvs]
    delta = functools.reduce(
        jnp.add,
        [jnp.sum(w.astype(jnp.float32) * d, axis=0, keepdims=True) for w, d in zip(weights, dprobs)],
    )
    dscores = [(p * (d - delta)).astype(jnp.bfloat16) for p, d in zip(probs, dprobs)]
    for distance, out in enumerate((own_ref, one_ref, two_ref)):
        out[:rows] = (nn(dscores[distance], q) * scale).astype(out.dtype)
        out[rows:] = nn(weights[distance], do).astype(out.dtype)
    dq_t = functools.reduce(
        jnp.add, [nn(kv[:rows].T, d) for kv, d in zip(kvs, dscores)]
    )
    dq_ref[...] = (dq_t.T * scale).astype(dq_ref.dtype)


def attention(shard, lengths, q, do, kv0, kv1, kv2):
    rows = q.shape[0]
    docs = lengths.shape[0]
    vmem = pl.BlockSpec(memory_space=pltpu.VMEM)
    pair = (2 * rows, DH)
    return pl.pallas_call(
        attention_kernel,
        out_shape=(
            jax.ShapeDtypeStruct((rows, DH), jnp.bfloat16),
            jax.ShapeDtypeStruct(pair, jnp.float32),
            jax.ShapeDtypeStruct(pair, jnp.bfloat16),
            jax.ShapeDtypeStruct(pair, jnp.bfloat16),
        ),
        in_specs=[pl.BlockSpec(memory_space=pltpu.SMEM)] + [vmem] * 7,
        out_specs=(vmem,) * 4,
        compiler_params=pltpu.CompilerParams(vmem_limit_bytes=40 * 1024 * 1024),
        name="attention",
    )(shard, lengths.reshape(1, docs), lengths.reshape(docs, 1), q, do, kv0, kv1, kv2)


def shards(queries, keys, values, d_out, lengths):
    rows = keys.shape[0]
    heads = lax.axis_size("head")
    part = rows // heads
    kv = jnp.concatenate([keys, values], axis=0)
    behind = [shifted(kv, "ctx", distance) for distance in range(1, SPAN + 1)]
    by_head = d_out.reshape(part, heads, DH).transpose(1, 0, 2)
    do = lax.all_to_all(by_head, "head", split_axis=0, concat_axis=0, tiled=True).reshape(rows, DH)
    shard = lax.axis_index("ctx").astype(jnp.int32).reshape(1)
    grad_queries, own, one, two = attention(shard, lengths, queries, do, kv, *behind)
    two = shifted(two, "ctx", -2)
    one = shifted(one, "ctx", -1)
    total = (own + one.astype(jnp.float32) + two.astype(jnp.float32)).astype(jnp.bfloat16)
    total = total.reshape(2, heads, part, DH).transpose(1, 0, 2, 3)
    shares = lax.all_to_all(total, "head", split_axis=0, concat_axis=0, tiled=True)
    share = jnp.sum(shares.astype(jnp.float32), axis=0).astype(jnp.bfloat16)
    return (grad_queries, share[0][None], share[1][None])


def solution(mesh):
    in_specs = (P("ctx", "head"), P("ctx", None), P("ctx", None), P("ctx", "head", None), P())
    out_specs = (P("ctx", "head"), P("ctx", "head", None), P("ctx", "head", None))
    return jax.shard_map(shards, mesh=mesh, in_specs=in_specs, out_specs=out_specs, check_vma=False)
```

time: 152 us -> 61.2 us (0.40)
  waiting for transfers between devices: 68.8 us -> 14.3 us
  matrix products: 14.8 us -> 0 us
  blocking collectives: 0 us -> 14.2 us
  between operations: 14.4 us -> 0.74 us
  starting transfers between devices: 35.7 us -> 24.6 us
  local copies, waits for them, and re-layouts: 11.9 us -> 3.07 us
  other arithmetic: 5.8 us -> 0.16 us
  Pallas kernels: 0 us -> 3.81 us
    reduce_scatter x2 -> x0, waiting for transfers between devices: 60.8 us -> none  [the longest x1 39.8 us: shards(): lax.psum_scatter(key_total[None], 'head', scatter_dimension=1, tiled=True)]
    dot_general x18 -> x0, matrix products: 14.8 us -> none  [the longest x3 4.12 us: shards(): jnp.einsum('htk,thd->kd', weight_tiles[distance], grad_rows, preferred_el...]
    all_to_all x0 -> x1, blocking collectives: none -> 14.2 us  [shards(): lax.all_to_all(total, 'head', split_axis=0, concat_axis=0, tiled=True)]
    ppermute x8 -> x4, starting transfers between devices: 28.4 us -> 17.4 us  [shifted(): lax.ppermute(value, axis, [(source, source + steps) for source in range(l...]
    unnamed x31 -> x10, local copies, waits for them, and re-layouts: 8.03 us -> 1.64 us
    all_to_all x1, waiting for transfers between devices: 4.45 us -> 8.27 us  [shards(): lax.all_to_all(by_head, 'head', split_axis=0, concat_axis=0, tiled=True)]
    pallas_call x0 -> x1, Pallas kernels: none -> 3.81 us  [attention(): pl.pallas_call(attention_kernel, out_shape=(jax.ShapeDtypeStruct((rows, D...]
    convert_element_type x3 -> x1, other arithmetic: 2.76 us -> 0.11 us  [shards(): (own + one.astype(jnp.float32) + two.astype(jnp.float32)).astype(jnp.bflo...]
  transfers between devices with their start and end apart: 11 -> 5, of which waited for: 4 -> 2; matrix products, arithmetic and copies ran while one was open for 18% -> 1% of each run, Pallas kernels for 0% -> 0%
where the time goes in v1:
time: 61.2 us; the launch traced here: 60.9 us
  starting transfers between devices  24.6 us (40%)
  waiting for transfers between devices  14.3 us (23%)
  blocking collectives  14.2 us (23%)
  Pallas kernels  3.81 us (6%)
  local copies, waits for them, and re-layouts  3.07 us (5%)
  between operations  0.74 us (1%)
    ppermute x4, starting transfers between devices, shifted(): lax.ppermute(value, axis, [(source, source + steps) for source in range(l...  17.4 us
    all_to_all x1, blocking collectives, shards(): lax.all_to_all(total, 'head', split_axis=0, concat_axis=0, tiled=True)  14.2 us
    all_to_all x1, waiting for transfers between devices, shards(): lax.all_to_all(by_head, 'head', split_axis=0, concat_axis=0, tiled=True)  8.27 us
    all_to_all x1, starting transfers between devices, shards(): lax.all_to_all(by_head, 'head', split_axis=0, concat_axis=0, tiled=True)  7.23 us
    ppermute x4, waiting for transfers between devices, shifted(): lax.ppermute(value, axis, [(source, source + steps) for source in range(l...  6.01 us
    pallas_call x1, Pallas kernels, attention(): pl.pallas_call(attention_kernel, out_shape=(jax.ShapeDtypeStruct((rows, D...  3.81 us
    unnamed x10, local copies, waits for them, and re-layouts  1.64 us
  transfers between devices with their start and end apart: 5, of which 2 were waited for; matrix products, arithmetic and copies ran while one was open for 1% of the time, Pallas kernels for 0%

profile of v1, /device:TPU:6, one launch (start us, length us, event | category | flops | bytes accessed | tf_op | source)
XLA Modules:
  0.0 60.9 jit_solution(11742044892445277712)
XLA Ops:
  0.6 0.0 copy-start.2
  0.6 0.9 %constant_dynamic-update-slice_fusion.1 = bf16[1024,128]{1,0:T(8,128)(2,1)S(1)} fusion(bf16[512,128]{1,0:T(8,128)(2,1)} %param.6), kind=kLoop, calls=%fused_computation.4 | loop fusion | bytes 262144
  1.6 0.0 copy-done.2
  1.6 0.0 copy-start.3
  1.6 4.4 %collective-permute-start.1 = (bf16[1024,128]{1,0:T(8,128)(2,1)S(1)}, bf16[1024,128]{1,0:T(8,128)(2,1)S(1)}, u32[]{:S(2)}, u32[]{:S(2)}) collective-permute-start(bf16[1024,128]{1,0:T(8,128)(2,1)S(1)} %constant_dynamic-update-slice_fusion.kv0_ref), channel_id=1, source_target_pairs={{0,2},{1,3},{2,4},{3,5},{4,6},{5,7},{6,8},{7,9},{8,10},{9,11},{10,... | collective-permute-start | bytes 786440 | tf_op jit(solution)/shard_map/ppermute | solution.py:18
  6.1 1.9 %collective-permute-start = (bf16[1024,128]{1,0:T(8,128)(2,1)S(1)}, bf16[1024,128]{1,0:T(8,128)(2,1)S(1)}, u32[]{:S(2)}, u32[]{:S(2)}) collective-permute-start(bf16[1024,128]{1,0:T(8,128)(2,1)S(1)} %constant_dynamic-update-slice_fusion.kv0_ref), channel_id=1, source_target_pairs={{0,1},{1,2},{2,3},{3,4},{4,5},{5,6},{6,7},{7,8},{8,9},{9,10},{10,1... | collective-permute-start | bytes 786440 | tf_op jit(solution)/shard_map/ppermute | solution.py:18
  8.0 0.0 copy-done.3
  8.0 0.7 %copy.17 = bf16[64,8,128]{2,0,1:T(8,128)(2,1)} copy(bf16[64,8,128]{2,1,0:T(8,128)(2,1)S(1)} %bitcast.19) | data formatting | bytes 262144 | tf_op jit(solution)/shard_map/reshape | solution.py:99
  8.7 0.0 copy-start
  8.7 7.2 %all-to-all-start = ((bf16[8,64,128]{2,1,0:T(8,128)(2,1)}), bf16[8,64,128]{2,1,0:T(8,128)(2,1)S(1)}, u32[]{:S(2)}, u32[]{:S(2)}) async-start(bf16[8,64,128]{2,1,0:T(8,128)(2,1)} %bitcast.13), calls=%async_computation | async-start | bytes 262144 | tf_op jit(solution)/shard_map/all_to_all | solution.py:100
  15.9 0.0 copy-start.1
  15.9 0.7 %copy-done.1 = s32[64]{0:T(128)S(1)} copy-done((s32[64]{0:T(128)S(1)}, s32[64]{0:T(128)}, u32[]{:S(2)}) %copy-start.1) | copy-done | bytes 280
  16.6 0.1 copy.11.len_col_ref
  16.7 8.3 %all-to-all-done = bf16[8,64,128]{2,1,0:T(8,128)(2,1)S(1)} async-done(((bf16[8,64,128]{2,1,0:T(8,128)(2,1)}), bf16[8,64,128]{2,1,0:T(8,128)(2,1)S(1)}, u32[]{:S(2)}, u32[]{:S(2)}) %all-to-all-start) | async-done | bytes 131104 | tf_op jit(solution)/shard_map/all_to_all | solution.py:100
  25.0 0.0 collective-permute-done.1.kv2_ref
  25.0 0.0 collective-permute-done.kv1_ref
  25.0 0.0 copy-done
  25.0 3.8 %attention.1 = (bf16[512,128]{1,0:T(8,128)(2,1)}, f32[1024,128]{1,0:T(8,128)S(1)}, bf16[1024,128]{1,0:T(8,128)(2,1)S(1)}, bf16[1024,128]{1,0:T(8,128)(2,1)S(1)}) custom-call(s32[1]{0:T(128)} %bitcast.shard_ref, s32[1,64]{1,0:T(1,128)S(1)} %bitcast.16, s32[64,1]{1,0:T(8,128)S(1)} %copy.11.len_col_ref, bf16[512,128]{1,0:T(8,128)(2,1)S(1)} %copy-done, ...), custom_call_target="tpu_custom_call" | custom-call | tf_op jit(solution)/shard_map/attention/pallas_call | solution.py:78
  28.8 6.8 %collective-permute-start.2 = (bf16[1024,128]{1,0:T(8,128)(2,1)S(1)}, bf16[1024,128]{1,0:T(8,128)(2,1)S(1)}, u32[]{:S(2)}, u32[]{:S(2)}) collective-permute-start(bf16[1024,128]{1,0:T(8,128)(2,1)S(1)} %get-tuple-element.9), channel_id=1, source_target_pairs={{1,0},{2,1},{3,2},{4,3},{5,4},{6,5},{7,6},{8,7},{9,8},{10,9},{11,1... | collective-permute-start | bytes 786440 | tf_op jit(solution)/shard_map/ppermute | solution.py:18
  35.5 4.3 %collective-permute-start.3 = (bf16[1024,128]{1,0:T(8,128)(2,1)S(1)}, bf16[1024,128]{1,0:T(8,128)(2,1)S(1)}, u32[]{:S(2)}, u32[]{:S(2)}) collective-permute-start(bf16[1024,128]{1,0:T(8,128)(2,1)S(1)} %get-tuple-element.10), channel_id=1, source_target_pairs={{2,0},{3,1},{4,2},{5,3},{6,4},{7,5},{8,6},{9,7},{10,8},{11,9},{12,... | collective-permute-start | bytes 786440 | tf_op jit(solution)/shard_map/ppermute | solution.py:18
  39.8 0.0 collective-permute-done.2
  39.8 6.0 %collective-permute-done.3 = bf16[1024,128]{1,0:T(8,128)(2,1)S(1)} collective-permute-done((bf16[1024,128]{1,0:T(8,128)(2,1)S(1)}, bf16[1024,128]{1,0:T(8,128)(2,1)S(1)}, u32[]{:S(2)}, u32[]{:S(2)}) %collective-permute-start.3) | collective-permute-done | bytes 262176 | tf_op jit(solution)/shard_map/ppermute | solution.py:18
  45.8 0.1 add_convert_fusion
  46.0 14.2 %all_to_all.10 = bf16[8,2,64,128]{3,2,1,0:T(8,128)(2,1)S(1)} all-to-all(bf16[8,2,64,128]{3,2,1,0:T(8,128)(2,1)S(1)} %bitcast.18), channel_id=1, replica_groups=mesh['head'=8,'ctx'=64] {'head'}, dimensions={0} | all-to-all | bytes 524288 | tf_op jit(solution)/shard_map/all_to_all | solution.py:107
  60.3 0.6 %fusion = (bf16[1,64,128]{2,1,0:T(8,128)(2,1)}, bf16[1,64,128]{2,1,0:T(8,128)(2,1)}) fusion(bf16[2,64,128]{2,1,0:T(8,128)(2,1)S(1)} %reduce_sum.12), kind=kLoop, calls=%fused_computation.5 | loop fusion | bytes 65536 | tf_op jit(solution)/shard_map/slice | solution.py:109
  (4 shorter events, 0.1 us)
Async XLA Ops:
  0.6 1.0 %copy-start.2 = (bf16[512,128]{1,0:T(8,128)(2,1)S(1)}, bf16[512,128]{1,0:T(8,128)(2,1)}, u32[]{:S(2)}) copy-start(bf16[512,128]{1,0:T(8,128)(2,1)} %param.7) | copy-start | bytes 393220
  1.6 6.4 %copy-start.3 = (bf16[1,64,1024]{2,1,0:T(8,128)(2,1)S(1)}, bf16[1,64,1024]{2,1,0:T(8,128)(2,1)}, u32[]{:S(2)}) copy-start(bf16[1,64,1024]{2,1,0:T(8,128)(2,1)} %param.8) | copy-start | bytes 393220
  1.6 23.3 %collective-permute-start.1 = (bf16[1024,128]{1,0:T(8,128)(2,1)S(1)}, bf16[1024,128]{1,0:T(8,128)(2,1)S(1)}, u32[]{:S(2)}, u32[]{:S(2)}) collective-permute-start(bf16[1024,128]{1,0:T(8,128)(2,1)S(1)} %constant_dynamic-update-slice_fusion.kv0_ref), channel_id=1, source_target_pairs={{0,2},{1,3},{2,4},{3,5},{4,6},{5,7},{6,8},{7,9},{8,10},{9,11},{10,... | collective-permute-start | bytes 786440 | tf_op jit(solution)/shard_map/ppermute | solution.py:18
  6.1 18.9 %collective-permute-start = (bf16[1024,128]{1,0:T(8,128)(2,1)S(1)}, bf16[1024,128]{1,0:T(8,128)(2,1)S(1)}, u32[]{:S(2)}, u32[]{:S(2)}) collective-permute-start(bf16[1024,128]{1,0:T(8,128)(2,1)S(1)} %constant_dynamic-update-slice_fusion.kv0_ref), channel_id=1, source_target_pairs={{0,1},{1,2},{2,3},{3,4},{4,5},{5,6},{6,7},{7,8},{8,9},{9,10},{10,1... | collective-permute-start | bytes 786440 | tf_op jit(solution)/shard_map/ppermute | solution.py:18
  8.7 16.3 %copy-start = (bf16[512,128]{1,0:T(8,128)(2,1)S(1)}, bf16[512,128]{1,0:T(8,128)(2,1)}, u32[]{:S(2)}) copy-start(bf16[512,128]{1,0:T(8,128)(2,1)} %q_ref.1) | copy-start | bytes 393220
  8.7 16.3 %all-to-all-start = ((bf16[8,64,128]{2,1,0:T(8,128)(2,1)}), bf16[8,64,128]{2,1,0:T(8,128)(2,1)S(1)}, u32[]{:S(2)}, u32[]{:S(2)}) async-start(bf16[8,64,128]{2,1,0:T(8,128)(2,1)} %bitcast.13), calls=%async_computation | async-start | bytes 262144 | tf_op jit(solution)/shard_map/all_to_all | solution.py:100
  15.9 0.7 %copy-start.1 = (s32[64]{0:T(128)S(1)}, s32[64]{0:T(128)}, u32[]{:S(2)}) copy-start(s32[64]{0:T(128)} %param.9) | copy-start | bytes 772
  28.8 11.0 %collective-permute-start.2 = (bf16[1024,128]{1,0:T(8,128)(2,1)S(1)}, bf16[1024,128]{1,0:T(8,128)(2,1)S(1)}, u32[]{:S(2)}, u32[]{:S(2)}) collective-permute-start(bf16[1024,128]{1,0:T(8,128)(2,1)S(1)} %get-tuple-element.9), channel_id=1, source_target_pairs={{1,0},{2,1},{3,2},{4,3},{5,4},{6,5},{7,6},{8,7},{9,8},{10,9},{11,1... | collective-permute-start | bytes 786440 | tf_op jit(solution)/shard_map/ppermute | solution.py:18
  35.5 10.3 %collective-permute-start.3 = (bf16[1024,128]{1,0:T(8,128)(2,1)S(1)}, bf16[1024,128]{1,0:T(8,128)(2,1)S(1)}, u32[]{:S(2)}, u32[]{:S(2)}) collective-permute-start(bf16[1024,128]{1,0:T(8,128)(2,1)S(1)} %get-tuple-element.10), channel_id=1, source_target_pairs={{2,0},{3,1},{4,2},{5,3},{6,4},{7,5},{8,6},{9,7},{10,8},{11,9},{12,... | collective-permute-start | bytes 786440 | tf_op jit(solution)/shard_map/ppermute | solution.py:18

commit v2 on v1

v2 whole, which is shorter than its diff:
```python
import functools

import jax
import jax.numpy as jnp
from jax import lax
from jax.experimental import pallas as pl
from jax.experimental.pallas import tpu as pltpu
from jax.sharding import PartitionSpec as P

DH = 128
SPAN = 2
LOG2E = 1.4426950408889634
SCALE = DH ** (-0.5)
VMEM = pl.BlockSpec(memory_space=pltpu.VMEM)
SMEM = pl.BlockSpec(memory_space=pltpu.SMEM)


def shifted(value, axis, steps):
    count = lax.axis_size(axis)
    leading, last = (max(0, -steps), min(count, count - steps))
    return lax.ppermute(value, axis, [(source, source + steps) for source in range(leading, last)])


def nt(a, b):
    return lax.dot_general(a, b, (((1,), (1,)), ((), ())), preferred_element_type=jnp.float32)


def nn(a, b):
    return lax.dot_general(a, b, (((1,), (0,)), ((), ())), preferred_element_type=jnp.float32)


def starts_of(len_ref, first, count):
    docs = len_ref.shape[1]
    j = lax.broadcasted_iota(jnp.int32, (docs, docs), 0)
    k = lax.broadcasted_iota(jnp.int32, (docs, docs), 1)
    ends = jnp.sum(jnp.where(k <= j, len_ref[...], 0), axis=1, keepdims=True)
    lens = jnp.sum(jnp.where(k == j, len_ref[...], 0), axis=1, keepdims=True)
    pos = first + lax.broadcasted_iota(jnp.int32, (1, count), 1)
    return jnp.sum(jnp.where(ends <= pos, lens, 0), axis=0, keepdims=True)


def masked(plain, start, key_first, causal):
    sub = lax.broadcasted_iota(jnp.int32, plain.shape, 0)
    seen = sub >= start - key_first
    if causal:
        seen = seen & (sub <= lax.broadcasted_iota(jnp.int32, plain.shape, 1))
    return jnp.where(seen, plain * (SCALE * LOG2E), -1e30)


def softmax_kernel(shard_ref, len_ref, q_ref, kv0_ref, kv1_ref, kv2_ref, weight_ref, start_ref, lse_ref):
    rows = q_ref.shape[0]
    first = shard_ref[0] * rows
    start = starts_of(len_ref, first, rows)
    q = q_ref[...]
    scores = [
        masked(nt(kv[:rows], q), start, first - distance * rows, distance == 0)
        for distance, kv in enumerate((kv0_ref, kv1_ref, kv2_ref))
    ]
    highest = functools.reduce(jnp.maximum, [jnp.max(s, axis=0, keepdims=True) for s in scores])
    probs = [jnp.exp2(s - highest) for s in scores]
    total = functools.reduce(jnp.add, [jnp.sum(p, axis=0, keepdims=True) for p in probs])
    inverse = 1.0 / total
    start_ref[...] = start
    lse_ref[...] = highest + jnp.log2(total)
    for distance in range(SPAN + 1):
        weight_ref[distance] = (probs[distance] * inverse).astype(jnp.bfloat16)


def far_kernel(weight_ref, q_ref, do_ref, kv0_ref, kv1_ref, kv2_ref, one_ref, two_ref, delta_ref):
    rows = do_ref.shape[0]
    q = q_ref[...]
    do = do_ref[...]
    dprobs = [nt(kv[rows:], do) for kv in (kv0_ref, kv1_ref, kv2_ref)]
    weights = [weight_ref[distance] for distance in range(SPAN + 1)]
    delta = functools.reduce(
        jnp.add,
        [jnp.sum(w.astype(jnp.float32) * d, axis=0, keepdims=True) for w, d in zip(weights, dprobs)],
    )
    delta_ref[...] = delta
    for distance, out_ref in ((2, two_ref), (1, one_ref)):
        dscore = (weights[distance].astype(jnp.float32) * (dprobs[distance] - delta)).astype(jnp.bfloat16)
        out_ref[:rows] = nn(dscore, q).astype(jnp.bfloat16)
        out_ref[rows:] = nn(weights[distance], do).astype(jnp.bfloat16)


def own_kernel(shard_ref, start_ref, lse_ref, delta_ref, q_ref, do_ref, kv0_ref, kv1_ref, kv2_ref, dq_ref, own_ref):
    rows = q_ref.shape[0]
    first = shard_ref[0] * rows
    q = q_ref[...]
    do = do_ref[...]
    dq_t = jnp.zeros((DH, rows), jnp.float32)
    for distance, kv in enumerate((kv0_ref, kv1_ref, kv2_ref)):
        score = masked(nt(kv[:rows], q), start_ref[...], first - distance * rows, distance == 0)
        prob = jnp.exp2(score - lse_ref[...])
        dscore = (prob * (nt(kv[rows:], do) - delta_ref[...])).astype(jnp.bfloat16)
        dq_t = dq_t + nn(kv[:rows].T, dscore)
        if distance == 0:
            own_ref[:rows] = nn(dscore, q)
            own_ref[rows:] = nn(prob.astype(jnp.bfloat16), do)
    dq_ref[...] = (dq_t.T * SCALE).astype(dq_ref.dtype)


def sum_kernel(own_ref, two_ref, one_ref, out_ref):
    rows = own_ref.shape[0] // 2
    heads, _, part, _ = out_ref.shape
    total = own_ref[...] + one_ref[...].astype(jnp.float32) + two_ref[...].astype(jnp.float32)
    out_ref[:, 0] = (total[:rows] * SCALE).astype(jnp.bfloat16).reshape(heads, part, DH)
    out_ref[:, 1] = total[rows:].astype(jnp.bfloat16).reshape(heads, part, DH)


def call(kernel, name, out_shape, in_specs, tiles, *operands):
    return pl.pallas_call(
        kernel,
        out_shape=out_shape,
        in_specs=in_specs,
        out_specs=jax.tree.map(lambda _: VMEM, out_shape),
        compiler_params=pltpu.CompilerParams(vmem_limit_bytes=20 * 1024 * 1024),
        cost_estimate=pl.CostEstimate(
            flops=tiles * 2 * 512 * 512 * DH, bytes_accessed=1 << 20, transcendentals=tiles * 512 * 512
        ),
        name=name,
    )(*operands)


def shards(queries, keys, values, d_out, lengths):
    rows = keys.shape[0]
    heads = lax.axis_size("head")
    part = rows // heads
    docs = lengths.shape[0]
    shape = jax.ShapeDtypeStruct
    pair = (2 * rows, DH)
    zero = jnp.zeros((), keys.dtype)
    groups = part // 8
    tiles = d_out.reshape(groups, 8, heads, DH).transpose(0, 2, 1, 3).reshape(rows, DH)
    kv = lax.pad(keys, zero, ((0, rows, 0), (0, 0, 0))) + lax.pad(values, zero, ((rows, 0, 0), (0, 0, 0)))
    by_head = tiles.reshape(groups, heads, 8, DH).transpose(1, 0, 2, 3).reshape(heads, part, DH)
    kv2 = shifted(kv, "ctx", 2)
    kv1 = shifted(kv, "ctx", 1)
    do = lax.all_to_all(by_head, "head", split_axis=0, concat_axis=0, tiled=True).reshape(rows, DH)
    shard = lax.axis_index("ctx").astype(jnp.int32).reshape(1)
    weights, start, lse = call(
        softmax_kernel,
        "softmax",
        (
            shape((SPAN + 1, rows, rows), jnp.bfloat16),
            shape((1, rows), jnp.int32),
            shape((1, rows), jnp.float32),
        ),
        [SMEM] + [VMEM] * 5,
        6,
        shard, lengths.reshape(1, docs), queries, kv, kv1, kv2,
    )
    one, two, delta = call(
        far_kernel,
        "far",
        (shape(pair, jnp.bfloat16), shape(pair, jnp.bfloat16), shape((1, rows), jnp.float32)),
        [VMEM] * 6,
        7,
        weights, queries, do, kv, kv1, kv2,
    )
    two = shifted(two, "ctx", -2)
    one = shifted(one, "ctx", -1)
    grad_queries, own = call(
        own_kernel,
        "own",
        (shape((rows, DH), jnp.bfloat16), shape(pair, jnp.float32)),
        [SMEM] + [VMEM] * 8,
        11,
        shard, start, lse, delta, queries, do, kv, kv1, kv2,
    )
    total = call(sum_kernel, "total", shape((heads, 2, part, DH), jnp.bfloat16), [VMEM] * 3, 1, own, two, one)
    shares = lax.all_to_all(total, "head", split_axis=0, concat_axis=0, tiled=True)
    share = jnp.sum(shares.astype(jnp.float32), axis=0).astype(jnp.bfloat16)
    return (grad_queries, share[0][None], share[1][None])


def solution(mesh):
    in_specs = (P("ctx", "head"), P("ctx", None), P("ctx", None), P("ctx", "head", None), P())
    out_specs = (P("ctx", "head"), P("ctx", "head", None), P("ctx", "head", None))
    return jax.shard_map(shards, mesh=mesh, in_specs=in_specs, out_specs=out_specs, check_vma=False)
```

time: 61.2 us -> 57.3 us (0.936)
  waiting for transfers between devices: 14.3 us -> 8.39 us
  Pallas kernels: 3.81 us -> 5.49 us
  other arithmetic: 0.16 us -> 1.06 us
    all_to_all x1, waiting for transfers between devices: 8.27 us -> 0.01 us  [shards(): lax.all_to_all(by_head, 'head', split_axis=0, concat_axis=0, tiled=True)]
    ppermute x4, waiting for transfers between devices: 6.01 us -> 8.39 us  [shifted(): lax.ppermute(value, axis, [(source, source + steps) for source in range(l...]
    pallas_call x1 -> x4, Pallas kernels: 3.81 us -> 5.49 us  [call(): pl.pallas_call(kernel, out_shape=out_shape, in_specs=in_specs, out_specs=...]
    add x0 -> x1, other arithmetic: none -> 1.02 us  [shards(): lax.pad(keys, zero, ((0, rows, 0), (0, 0, 0)))]
    unnamed x10 -> x8, local copies, waits for them, and re-layouts: 1.64 us -> 1.57 us
  transfers between devices with their start and end apart: 5 -> 5, of which waited for: 2 -> 3; matrix products, arithmetic and copies ran while one was open for 1% -> 1% of each run, Pallas kernels for 0% -> 7%
where the time goes in v2:
time: 57.3 us; the launch traced here: 57 us
  starting transfers between devices  24.2 us (42%)
  blocking collectives  14.3 us (25%)
  waiting for transfers between devices  8.39 us (15%)
  Pallas kernels  5.49 us (10%)
  local copies, waits for them, and re-layouts  2.87 us (5%)
  other arithmetic  1.06 us (2%)
  between operations  0.72 us (1%)
    ppermute x4, starting transfers between devices, shifted(): lax.ppermute(value, axis, [(source, source + steps) for source in range(l...  16.9 us
    all_to_all x1, blocking collectives, shards(): lax.all_to_all(total, 'head', split_axis=0, concat_axis=0, tiled=True)  14.3 us
    ppermute x4, waiting for transfers between devices, shifted(): lax.ppermute(value, axis, [(source, source + steps) for source in range(l...  8.39 us
    all_to_all x1, starting transfers between devices, shards(): lax.all_to_all(by_head, 'head', split_axis=0, concat_axis=0, tiled=True)  7.23 us
    pallas_call x4, Pallas kernels, call(): pl.pallas_call(kernel, out_shape=out_shape, in_specs=in_specs, out_specs=...  5.49 us
    unnamed x8, local copies, waits for them, and re-layouts  1.57 us
  transfers between devices with their start and end apart: 5, of which 3 were waited for; matrix products, arithmetic and copies ran while one was open for 1% of the time, Pallas kernels for 7%

profile of v2, /device:TPU:6, one launch (start us, length us, event | category | flops | bytes accessed | tf_op | source)
XLA Modules:
  0.0 57.0 jit_solution(6280112393022937807)
XLA Ops:
  0.6 0.0 copy-start
  0.6 1.0 %pad_add_fusion.kv0_ref = bf16[1024,128]{1,0:T(8,128)(2,1)S(1)} fusion(bf16[512,128]{1,0:T(8,128)(2,1)} %param.7, bf16[512,128]{1,0:T(8,128)(2,1)} %param.6), kind=kLoop, calls=%fused_computation | loop fusion | flops 524288 | bytes 524288 | tf_op jit(solution)/shard_map/add | solution.py:135
  1.7 4.3 %collective-permute-start.1 = (bf16[1024,128]{1,0:T(8,128)(2,1)S(1)}, bf16[1024,128]{1,0:T(8,128)(2,1)S(1)}, u32[]{:S(2)}, u32[]{:S(2)}) collective-permute-start(bf16[1024,128]{1,0:T(8,128)(2,1)S(1)} %pad_add_fusion.kv0_ref), channel_id=1, source_target_pairs={{0,2},{1,3},{2,4},{3,5},{4,6},{5,7},{6,8},{7,9},{8,10},{9,11},{10,... | collective-permute-start | bytes 786440 | tf_op jit(solution)/shard_map/ppermute | solution.py:21
  6.0 1.9 %collective-permute-start = (bf16[1024,128]{1,0:T(8,128)(2,1)S(1)}, bf16[1024,128]{1,0:T(8,128)(2,1)S(1)}, u32[]{:S(2)}, u32[]{:S(2)}) collective-permute-start(bf16[1024,128]{1,0:T(8,128)(2,1)S(1)} %pad_add_fusion.kv0_ref), channel_id=1, source_target_pairs={{0,1},{1,2},{2,3},{3,4},{4,5},{5,6},{6,7},{7,8},{8,9},{9,10},{10,1... | collective-permute-start | bytes 786440 | tf_op jit(solution)/shard_map/ppermute | solution.py:21
  7.9 0.0 copy-done
  7.9 0.7 %copy_bitcast_fusion = bf16[8,64,128]{2,1,0:T(8,128)(2,1)} fusion(bf16[1,64,1024]{2,1,0:T(8,128)(2,1)S(1)} %copy-done), kind=kLoop, calls=%fused_computation.1 | loop fusion | bytes 262144 | tf_op jit(solution)/shard_map/reshape | solution.py:136
  8.6 0.0 copy-start.2
  8.6 7.2 %all-to-all-start = ((bf16[8,64,128]{2,1,0:T(8,128)(2,1)}), bf16[8,64,128]{2,1,0:T(8,128)(2,1)S(1)}, u32[]{:S(2)}, u32[]{:S(2)}) async-start(bf16[8,64,128]{2,1,0:T(8,128)(2,1)} %copy_bitcast_fusion), calls=%async_computation | async-start | bytes 262144 | tf_op jit(solution)/shard_map/all_to_all | solution.py:139
  15.8 4.2 %collective-permute-done.1.kv2_ref = bf16[1024,128]{1,0:T(8,128)(2,1)S(1)} collective-permute-done((bf16[1024,128]{1,0:T(8,128)(2,1)S(1)}, bf16[1024,128]{1,0:T(8,128)(2,1)S(1)}, u32[]{:S(2)}, u32[]{:S(2)}) %collective-permute-start.1) | collective-permute-done | bytes 262176 | tf_op jit(solution)/shard_map/ppermute | solution.py:21
  20.0 2.0 %collective-permute-done.kv1_ref = bf16[1024,128]{1,0:T(8,128)(2,1)S(1)} collective-permute-done((bf16[1024,128]{1,0:T(8,128)(2,1)S(1)}, bf16[1024,128]{1,0:T(8,128)(2,1)S(1)}, u32[]{:S(2)}, u32[]{:S(2)}) %collective-permute-start) | collective-permute-done | bytes 262176 | tf_op jit(solution)/shard_map/ppermute | solution.py:21
  22.0 0.0 copy-start.1
  22.0 0.9 %copy-done.1 = bf16[512,128]{1,0:T(8,128)(2,1)S(1)} copy-done((bf16[512,128]{1,0:T(8,128)(2,1)S(1)}, bf16[512,128]{1,0:T(8,128)(2,1)}, u32[]{:S(2)}) %copy-start.1) | copy-done | bytes 131096
  22.9 0.0 copy-start.3
  22.9 0.7 %copy-done.3 = s32[64]{0:T(128)S(1)} copy-done((s32[64]{0:T(128)S(1)}, s32[64]{0:T(128)}, u32[]{:S(2)}) %copy-start.3) | copy-done | bytes 280
  23.6 1.4 %softmax.1 = (bf16[3,512,512]{2,1,0:T(8,128)(2,1)S(1)}, s32[1,512]{1,0:T(1,128)S(1)}, f32[1,512]{1,0:T(1,128)S(1)}) custom-call(s32[1]{0:T(128)} %bitcast.shard_ref, s32[1,64]{1,0:T(1,128)S(1)} %bitcast.12, bf16[512,128]{1,0:T(8,128)(2,1)S(1)} %copy-done.1, bf16[1024,128]{1,0:T(8,128)(2,1)S(1)} %pad_add_fusion.kv0_ref, ...), custom_call_target="tpu_custom_call" | custom-call | flops 402653184 | bytes 1048576 | tf_op jit(solution)/shard_map/softmax/pallas_call | solution.py:112
  24.9 0.0 all-to-all-done
  24.9 0.0 copy-done.2
  25.0 1.4 %far.1 = (bf16[1024,128]{1,0:T(8,128)(2,1)S(1)}, bf16[1024,128]{1,0:T(8,128)(2,1)S(1)}, f32[1,512]{1,0:T(1,128)S(1)}) custom-call(bf16[3,512,512]{2,1,0:T(8,128)(2,1)S(1)} %get-tuple-element.13.weight_ref, bf16[512,128]{1,0:T(8,128)(2,1)S(1)} %copy-done.2, bf16[512,128]{1,0:T(8,128)(2,1)S(1)} %bitcast.10, bf16[1024,128]{1,0:T(8,128)(2,1)S(1)} %pad_add_fusion.kv0_ref, ...), custom_call_target="tpu_custom_call" | custom-call | flops 469762048 | bytes 1048576 | tf_op jit(solution)/shard_map/far/pallas_call | solution.py:112
  26.4 8.8 %collective-permute-start.2 = (bf16[1024,128]{1,0:T(8,128)(2,1)S(1)}, bf16[1024,128]{1,0:T(8,128)(2,1)S(1)}, u32[]{:S(2)}, u32[]{:S(2)}) collective-permute-start(bf16[1024,128]{1,0:T(8,128)(2,1)S(1)} %get-tuple-element.17), channel_id=1, source_target_pairs={{2,0},{3,1},{4,2},{5,3},{6,4},{7,5},{8,6},{9,7},{10,8},{11,9},{12,... | collective-permute-start | bytes 786440 | tf_op jit(solution)/shard_map/ppermute | solution.py:21
  35.2 1.9 %collective-permute-start.3 = (bf16[1024,128]{1,0:T(8,128)(2,1)S(1)}, bf16[1024,128]{1,0:T(8,128)(2,1)S(1)}, u32[]{:S(2)}, u32[]{:S(2)}) collective-permute-start(bf16[1024,128]{1,0:T(8,128)(2,1)S(1)} %get-tuple-element.18), channel_id=1, source_target_pairs={{1,0},{2,1},{3,2},{4,3},{5,4},{6,5},{7,6},{8,7},{9,8},{10,9},{11,1... | collective-permute-start | bytes 786440 | tf_op jit(solution)/shard_map/ppermute | solution.py:21
  37.1 2.6 %own.1 = (bf16[512,128]{1,0:T(8,128)(2,1)}, f32[1024,128]{1,0:T(8,128)S(1)}) custom-call(s32[1]{0:T(128)} %bitcast.shard_ref, s32[1,512]{1,0:T(1,128)S(1)} %get-tuple-element.11.start_ref, f32[1,512]{1,0:T(1,128)S(1)} %get-tuple-element.12.lse_ref, f32[1,512]{1,0:T(1,128)S(1)} %get-tuple-element.14.delta_ref, bf16[512,128]{1,0:T(8,128)(2,1)S(1)} %copy-done.2, ...), custom_call_target="tpu_custom_call" | custom-call | flops 738197504 | bytes 1048576 | tf_op jit(solution)/shard_map/own/pallas_call | solution.py:112
  39.7 0.0 collective-permute-done.2.two_ref
  39.7 2.2 %collective-permute-done.3.one_ref = bf16[1024,128]{1,0:T(8,128)(2,1)S(1)} collective-permute-done((bf16[1024,128]{1,0:T(8,128)(2,1)S(1)}, bf16[1024,128]{1,0:T(8,128)(2,1)S(1)}, u32[]{:S(2)}, u32[]{:S(2)}) %collective-permute-start.3) | collective-permute-done | bytes 262176 | tf_op jit(solution)/shard_map/ppermute | solution.py:21
  41.9 0.1 total.1
  42.0 14.3 %all_to_all.10 = bf16[8,2,64,128]{3,2,1,0:T(8,128)(2,1)S(1)} all-to-all(bf16[8,2,64,128]{3,2,1,0:T(8,128)(2,1)S(1)} %total.1), channel_id=1, replica_groups=mesh['head'=8,'ctx'=64] {'head'}, dimensions={0} | all-to-all | bytes 524288 | tf_op jit(solution)/shard_map/all_to_all | solution.py:172
  56.4 0.6 %fusion = (bf16[1,64,128]{2,1,0:T(8,128)(2,1)}, bf16[1,64,128]{2,1,0:T(8,128)(2,1)}) fusion(bf16[2,64,128]{2,1,0:T(8,128)(2,1)S(1)} %reduce_sum.12), kind=kLoop, calls=%fused_computation.2 | loop fusion | bytes 65536 | tf_op jit(solution)/shard_map/slice | solution.py:174
  (1 shorter events, 0.0 us)
Async XLA Ops:
  0.6 7.3 %copy-start = (bf16[1,64,1024]{2,1,0:T(8,128)(2,1)S(1)}, bf16[1,64,1024]{2,1,0:T(8,128)(2,1)}, u32[]{:S(2)}) copy-start(bf16[1,64,1024]{2,1,0:T(8,128)(2,1)} %param.8) | copy-start | bytes 393220
  1.7 18.3 %collective-permute-start.1 = (bf16[1024,128]{1,0:T(8,128)(2,1)S(1)}, bf16[1024,128]{1,0:T(8,128)(2,1)S(1)}, u32[]{:S(2)}, u32[]{:S(2)}) collective-permute-start(bf16[1024,128]{1,0:T(8,128)(2,1)S(1)} %pad_add_fusion.kv0_ref), channel_id=1, source_target_pairs={{0,2},{1,3},{2,4},{3,5},{4,6},{5,7},{6,8},{7,9},{8,10},{9,11},{10,... | collective-permute-start | bytes 786440 | tf_op jit(solution)/shard_map/ppermute | solution.py:21
  6.0 16.0 %collective-permute-start = (bf16[1024,128]{1,0:T(8,128)(2,1)S(1)}, bf16[1024,128]{1,0:T(8,128)(2,1)S(1)}, u32[]{:S(2)}, u32[]{:S(2)}) collective-permute-start(bf16[1024,128]{1,0:T(8,128)(2,1)S(1)} %pad_add_fusion.kv0_ref), channel_id=1, source_target_pairs={{0,1},{1,2},{2,3},{3,4},{4,5},{5,6},{6,7},{7,8},{8,9},{9,10},{10,1... | collective-permute-start | bytes 786440 | tf_op jit(solution)/shard_map/ppermute | solution.py:21
  8.6 16.4 %copy-start.2 = (bf16[512,128]{1,0:T(8,128)(2,1)S(1)}, bf16[512,128]{1,0:T(8,128)(2,1)}, u32[]{:S(2)}) copy-start(bf16[512,128]{1,0:T(8,128)(2,1)} %q_ref.5) | copy-start | bytes 393220
  8.6 16.4 %all-to-all-start = ((bf16[8,64,128]{2,1,0:T(8,128)(2,1)}), bf16[8,64,128]{2,1,0:T(8,128)(2,1)S(1)}, u32[]{:S(2)}, u32[]{:S(2)}) async-start(bf16[8,64,128]{2,1,0:T(8,128)(2,1)} %copy_bitcast_fusion), calls=%async_computation | async-start | bytes 262144 | tf_op jit(solution)/shard_map/all_to_all | solution.py:139
  22.0 0.9 %copy-start.1 = (bf16[512,128]{1,0:T(8,128)(2,1)S(1)}, bf16[512,128]{1,0:T(8,128)(2,1)}, u32[]{:S(2)}) copy-start(bf16[512,128]{1,0:T(8,128)(2,1)} %q_ref.5) | copy-start | bytes 393220
  22.9 0.7 %copy-start.3 = (s32[64]{0:T(128)S(1)}, s32[64]{0:T(128)}, u32[]{:S(2)}) copy-start(s32[64]{0:T(128)} %param.9) | copy-start | bytes 772
  26.4 13.3 %collective-permute-start.2 = (bf16[1024,128]{1,0:T(8,128)(2,1)S(1)}, bf16[1024,128]{1,0:T(8,128)(2,1)S(1)}, u32[]{:S(2)}, u32[]{:S(2)}) collective-permute-start(bf16[1024,128]{1,0:T(8,128)(2,1)S(1)} %get-tuple-element.17), channel_id=1, source_target_pairs={{2,0},{3,1},{4,2},{5,3},{6,4},{7,5},{8,6},{9,7},{10,8},{11,9},{12,... | collective-permute-start | bytes 786440 | tf_op jit(solution)/shard_map/ppermute | solution.py:21
  35.2 6.7 %collective-permute-start.3 = (bf16[1024,128]{1,0:T(8,128)(2,1)S(1)}, bf16[1024,128]{1,0:T(8,128)(2,1)S(1)}, u32[]{:S(2)}, u32[]{:S(2)}) collective-permute-start(bf16[1024,128]{1,0:T(8,128)(2,1)S(1)} %get-tuple-element.18), channel_id=1, source_target_pairs={{1,0},{2,1},{3,2},{4,3},{5,4},{6,5},{7,6},{8,7},{9,8},{10,9},{11,1... | collective-permute-start | bytes 786440 | tf_op jit(solution)/shard_map/ppermute | solution.py:21

commit v3 on v2

--- a/solution.py
+++ b/solution.py
@@ -47,10 +47,16 @@
     return jnp.where(seen, plain * (SCALE * LOG2E), -1e30)
 
 
-def softmax_kernel(shard_ref, len_ref, q_ref, kv0_ref, kv1_ref, kv2_ref, weight_ref, start_ref, lse_ref):
+def load_kernel(shard_ref, len_ref, q_ref, start_ref, out_ref):
+    rows = q_ref.shape[0]
+    start_ref[...] = starts_of(len_ref, shard_ref[0] * rows, rows)
+    out_ref[...] = q_ref[...]
+
+
+def softmax_kernel(shard_ref, start_ref, q_ref, kv0_ref, kv1_ref, kv2_ref, weight_ref, lse_ref):
     rows = q_ref.shape[0]
     first = shard_ref[0] * rows
-    start = starts_of(len_ref, first, rows)
+    start = start_ref[...]
     q = q_ref[...]
     scores = [
         masked(nt(kv[:rows], q), start, first - distance * rows, distance == 0)
@@ -60,27 +66,49 @@
     probs = [jnp.exp2(s - highest) for s in scores]
     total = functools.reduce(jnp.add, [jnp.sum(p, axis=0, keepdims=True) for p in probs])
     inverse = 1.0 / total
-    start_ref[...] = start
     lse_ref[...] = highest + jnp.log2(total)
     for distance in range(SPAN + 1):
         weight_ref[distance] = (probs[distance] * inverse).astype(jnp.bfloat16)
 
 
-def far_kernel(weight_ref, q_ref, do_ref, kv0_ref, kv1_ref, kv2_ref, one_ref, two_ref, delta_ref):
+def far_kernel(shard_ref, start_ref, weight_ref, q_ref, do_ref, kv0_ref, kv1_ref, kv2_ref,
+               one_ref, two_ref, delta_ref):
     rows = do_ref.shape[0]
     q = q_ref[...]
     do = do_ref[...]
-    dprobs = [nt(kv[rows:], do) for kv in (kv0_ref, kv1_ref, kv2_ref)]
-    weights = [weight_ref[distance] for distance in range(SPAN + 1)]
-    delta = functools.reduce(
-        jnp.add,
-        [jnp.sum(w.astype(jnp.float32) * d, axis=0, keepdims=True) for w, d in zip(weights, dprobs)],
-    )
-    delta_ref[...] = delta
-    for distance, out_ref in ((2, two_ref), (1, one_ref)):
-        dscore = (weights[distance].astype(jnp.float32) * (dprobs[distance] - delta)).astype(jnp.bfloat16)
-        out_ref[:rows] = nn(dscore, q).astype(jnp.bfloat16)
-        out_ref[rows:] = nn(weights[distance], do).astype(jnp.bfloat16)
+    half = rows // 2
+    reach = (shard_ref[0] - 1) * rows - jnp.min(start_ref[...])
+    near = nt(kv1_ref[rows:], do)
+    delta_ref[...] = jnp.sum(
+        weight_ref[0].astype(jnp.float32) * nt(kv0_ref[rows:], do), axis=0, keepdims=True
+    ) + jnp.sum(weight_ref[1].astype(jnp.float32) * near, axis=0, keepdims=True)
+
+    def farthest(keys_at, count):
+        weight = weight_ref[2, keys_at:, :count]
+        dprob = nt(kv2_ref[rows + keys_at :], do[:count])
+        delta = delta_ref[:, :count] + jnp.sum(weight.astype(jnp.float32) * dprob, axis=0, keepdims=True)
+        delta_ref[:, :count] = delta
+        dscore = (weight.astype(jnp.float32) * (dprob - delta)).astype(jnp.bfloat16)
+        two_ref[keys_at:rows] = nn(dscore, q[:count]).astype(jnp.bfloat16)
+        two_ref[rows + keys_at :] = nn(weight, do[:count]).astype(jnp.bfloat16)
+
+    @pl.when((reach > 0) & (reach <= half))
+    def _():
+        two_ref[:half] = jnp.zeros((half, DH), jnp.bfloat16)
+        two_ref[rows : rows + half] = jnp.zeros((half, DH), jnp.bfloat16)
+        farthest(half, rows)
+
+    @pl.when(reach > half)
+    def _():
+        farthest(0, half)
+
+    @pl.when(reach <= 0)
+    def _():
+        two_ref[...] = jnp.zeros_like(two_ref)
+
+    dscore = (weight_ref[1].astype(jnp.float32) * (near - delta_ref[...])).astype(jnp.bfloat16)
+    one_ref[:rows] = nn(dscore, q).astype(jnp.bfloat16)
+    one_ref[rows:] = nn(weight_ref[1], do).astype(jnp.bfloat16)
 
 
 def own_kernel(shard_ref, start_ref, lse_ref, delta_ref, q_ref, do_ref, kv0_ref, kv1_ref, kv2_ref, dq_ref, own_ref):
@@ -108,12 +136,13 @@
     out_ref[:, 1] = total[rows:].astype(jnp.bfloat16).reshape(heads, part, DH)
 
 
-def call(kernel, name, out_shape, in_specs, tiles, *operands):
+def call(kernel, name, out_shape, in_specs, tiles, *operands, scratch=()):
     return pl.pallas_call(
         kernel,
         out_shape=out_shape,
         in_specs=in_specs,
         out_specs=jax.tree.map(lambda _: VMEM, out_shape),
+        scratch_shapes=scratch,
         compiler_params=pltpu.CompilerParams(vmem_limit_bytes=20 * 1024 * 1024),
         cost_estimate=pl.CostEstimate(
             flops=tiles * 2 * 512 * 512 * DH, bytes_accessed=1 << 20, transcendentals=tiles * 512 * 512
@@ -138,25 +167,32 @@
     kv1 = shifted(kv, "ctx", 1)
     do = lax.all_to_all(by_head, "head", split_axis=0, concat_axis=0, tiled=True).reshape(rows, DH)
     shard = lax.axis_index("ctx").astype(jnp.int32).reshape(1)
-    weights, start, lse = call(
+    start, queries = call(
+        load_kernel,
+        "load",
+        (shape((1, rows), jnp.int32), shape((rows, DH), jnp.bfloat16)),
+        [SMEM] + [VMEM] * 2,
+        1,
+        shard, lengths.reshape(1, docs), queries,
+    )
+    weights, lse = call(
         softmax_kernel,
         "softmax",
         (
             shape((SPAN + 1, rows, rows), jnp.bfloat16),
-            shape((1, rows), jnp.int32),
             shape((1, rows), jnp.float32),
         ),
         [SMEM] + [VMEM] * 5,
         6,
-        shard, lengths.reshape(1, docs), queries, kv, kv1, kv2,
+        shard, start, queries, kv, kv1, kv2,
     )
     one, two, delta = call(
         far_kernel,
         "far",
         (shape(pair, jnp.bfloat16), shape(pair, jnp.bfloat16), shape((1, rows), jnp.float32)),
-        [VMEM] * 6,
+        [SMEM] + [VMEM] * 7,
         7,
-        weights, queries, do, kv, kv1, kv2,
+        shard, start, weights, queries, do, kv, kv1, kv2,
     )
     two = shifted(two, "ctx", -2)
     one = shifted(one, "ctx", -1)

time: 57.3 us -> 56.9 us (level)
  blocking collectives: 14.3 us -> 13.6 us
    ppermute x4, waiting for transfers between devices: 8.39 us -> 6.95 us  [shifted(): lax.ppermute(value, axis, [(source, source + steps) for source in range(l...]
    all_to_all x1, waiting for transfers between devices: 0.01 us -> 1.33 us  [shards(): lax.all_to_all(by_head, 'head', split_axis=0, concat_axis=0, tiled=True)]
    all_to_all x1, blocking collectives: 14.3 us -> 13.6 us  [shards(): lax.all_to_all(total, 'head', split_axis=0, concat_axis=0, tiled=True)]
    ppermute x4, starting transfers between devices: 16.9 us -> 17.5 us  [shifted(): lax.ppermute(value, axis, [(source, source + steps) for source in range(l...]
    pallas_call x4 -> x5, Pallas kernels: 5.49 us -> 5.13 us  [call(): pl.pallas_call(kernel, out_shape=out_shape, in_specs=in_specs, out_specs=...]
    unnamed x8 -> x6, local copies, waits for them, and re-layouts: 1.57 us -> 1.57 us
  transfers between devices with their start and end apart: 5 -> 5, of which waited for: 3 -> 4; matrix products, arithmetic and copies ran while one was open for 1% -> 1% of each run, Pallas kernels for 7% -> 7%
where the time goes in v3:
time: 56.9 us; the launch traced here: 56.3 us
  starting transfers between devices  24.6 us (43%)
  blocking collectives  13.6 us (24%)
  waiting for transfers between devices  8.29 us (15%)
  Pallas kernels  5.13 us (9%)
  local copies, waits for them, and re-layouts  2.86 us (5%)
  other arithmetic  1.06 us (2%)
  between operations  0.71 us (1%)
    ppermute x4, starting transfers between devices, shifted(): lax.ppermute(value, axis, [(source, source + steps) for source in range(l...  17.5 us
    all_to_all x1, blocking collectives, shards(): lax.all_to_all(total, 'head', split_axis=0, concat_axis=0, tiled=True)  13.6 us
    all_to_all x1, starting transfers between devices, shards(): lax.all_to_all(by_head, 'head', split_axis=0, concat_axis=0, tiled=True)  7.1 us
    ppermute x4, waiting for transfers between devices, shifted(): lax.ppermute(value, axis, [(source, source + steps) for source in range(l...  6.95 us
    pallas_call x5, Pallas kernels, call(): pl.pallas_call(kernel, out_shape=out_shape, in_specs=in_specs, out_specs=...  5.13 us
    unnamed x6, local copies, waits for them, and re-layouts  1.57 us
    all_to_all x1, waiting for transfers between devices, shards(): lax.all_to_all(by_head, 'head', split_axis=0, concat_axis=0, tiled=True)  1.33 us
  transfers between devices with their start and end apart: 5, of which 4 were waited for; matrix products, arithmetic and copies ran while one was open for 1% of the time, Pallas kernels for 7%

profile of v3, /device:TPU:6, one launch (start us, length us, event | category | flops | bytes accessed | tf_op | source)
XLA Modules:
  0.0 56.3 jit_solution(17501754517774380141)
XLA Ops:
  0.6 0.0 copy-start
  0.6 1.0 %pad_add_fusion.kv0_ref = bf16[1024,128]{1,0:T(8,128)(2,1)S(1)} fusion(bf16[512,128]{1,0:T(8,128)(2,1)} %param.7, bf16[512,128]{1,0:T(8,128)(2,1)} %param.6), kind=kLoop, calls=%fused_computation | loop fusion | flops 524288 | bytes 524288 | tf_op jit(solution)/shard_map/add | solution.py:164
  1.7 4.3 %collective-permute-start.1 = (bf16[1024,128]{1,0:T(8,128)(2,1)S(1)}, bf16[1024,128]{1,0:T(8,128)(2,1)S(1)}, u32[]{:S(2)}, u32[]{:S(2)}) collective-permute-start(bf16[1024,128]{1,0:T(8,128)(2,1)S(1)} %pad_add_fusion.kv0_ref), channel_id=1, source_target_pairs={{0,2},{1,3},{2,4},{3,5},{4,6},{5,7},{6,8},{7,9},{8,10},{9,11},{10,... | collective-permute-start | bytes 786440 | tf_op jit(solution)/shard_map/ppermute | solution.py:21
  6.0 1.9 %collective-permute-start = (bf16[1024,128]{1,0:T(8,128)(2,1)S(1)}, bf16[1024,128]{1,0:T(8,128)(2,1)S(1)}, u32[]{:S(2)}, u32[]{:S(2)}) collective-permute-start(bf16[1024,128]{1,0:T(8,128)(2,1)S(1)} %pad_add_fusion.kv0_ref), channel_id=1, source_target_pairs={{0,1},{1,2},{2,3},{3,4},{4,5},{5,6},{6,7},{7,8},{8,9},{9,10},{10,1... | collective-permute-start | bytes 786440 | tf_op jit(solution)/shard_map/ppermute | solution.py:21
  7.9 0.0 copy-done
  7.9 0.7 %copy_bitcast_fusion = bf16[8,64,128]{2,1,0:T(8,128)(2,1)} fusion(bf16[1,64,1024]{2,1,0:T(8,128)(2,1)S(1)} %copy-done), kind=kLoop, calls=%fused_computation.1 | loop fusion | bytes 262144 | tf_op jit(solution)/shard_map/reshape | solution.py:165
  8.6 7.1 %all-to-all-start = ((bf16[8,64,128]{2,1,0:T(8,128)(2,1)}), bf16[8,64,128]{2,1,0:T(8,128)(2,1)S(1)}, u32[]{:S(2)}, u32[]{:S(2)}) async-start(bf16[8,64,128]{2,1,0:T(8,128)(2,1)} %copy_bitcast_fusion), calls=%async_computation | async-start | bytes 262144 | tf_op jit(solution)/shard_map/all_to_all | solution.py:168
  15.7 0.0 copy-start.1
  15.7 0.9 %copy-done.1 = bf16[512,128]{1,0:T(8,128)(2,1)S(1)} copy-done((bf16[512,128]{1,0:T(8,128)(2,1)S(1)}, bf16[512,128]{1,0:T(8,128)(2,1)}, u32[]{:S(2)}) %copy-start.1) | copy-done | bytes 131096
  16.6 0.0 copy-start.2
  16.6 0.7 %copy-done.2 = s32[64]{0:T(128)S(1)} copy-done((s32[64]{0:T(128)S(1)}, s32[64]{0:T(128)}, u32[]{:S(2)}) %copy-start.2) | copy-done | bytes 280
  17.2 0.1 load.1
  17.4 2.6 %collective-permute-done.1.kv2_ref = bf16[1024,128]{1,0:T(8,128)(2,1)S(1)} collective-permute-done((bf16[1024,128]{1,0:T(8,128)(2,1)S(1)}, bf16[1024,128]{1,0:T(8,128)(2,1)S(1)}, u32[]{:S(2)}, u32[]{:S(2)}) %collective-permute-start.1) | collective-permute-done | bytes 262176 | tf_op jit(solution)/shard_map/ppermute | solution.py:21
  20.0 2.0 %collective-permute-done.kv1_ref = bf16[1024,128]{1,0:T(8,128)(2,1)S(1)} collective-permute-done((bf16[1024,128]{1,0:T(8,128)(2,1)S(1)}, bf16[1024,128]{1,0:T(8,128)(2,1)S(1)}, u32[]{:S(2)}, u32[]{:S(2)}) %collective-permute-start) | collective-permute-done | bytes 262176 | tf_op jit(solution)/shard_map/ppermute | solution.py:21
  22.0 1.4 %softmax.1 = (bf16[3,512,512]{2,1,0:T(8,128)(2,1)S(1)}, f32[1,512]{1,0:T(1,128)S(1)}) custom-call(s32[1]{0:T(128)} %bitcast.shard_ref, s32[1,512]{1,0:T(1,128)S(1)} %get-tuple-element.12.start_ref, bf16[512,128]{1,0:T(8,128)(2,1)S(1)} %get-tuple-element.13.q_ref, bf16[1024,128]{1,0:T(8,128)(2,1)S(1)} %pad_add_fusion.kv0_ref, ...), custom_call_target="tpu_custom_call" | custom-call | flops 402653184 | bytes 1048576 | tf_op jit(solution)/shard_map/softmax/pallas_call | solution.py:140
  23.4 1.3 %all-to-all-done = bf16[8,64,128]{2,1,0:T(8,128)(2,1)S(1)} async-done(((bf16[8,64,128]{2,1,0:T(8,128)(2,1)}), bf16[8,64,128]{2,1,0:T(8,128)(2,1)S(1)}, u32[]{:S(2)}, u32[]{:S(2)}) %all-to-all-start) | async-done | bytes 131104 | tf_op jit(solution)/shard_map/all_to_all | solution.py:168
  24.7 0.9 %far.1 = (bf16[1024,128]{1,0:T(8,128)(2,1)S(1)}, bf16[1024,128]{1,0:T(8,128)(2,1)S(1)}, f32[1,512]{1,0:T(1,128)S(1)}) custom-call(s32[1]{0:T(128)} %bitcast.shard_ref, s32[1,512]{1,0:T(1,128)S(1)} %get-tuple-element.12.start_ref, bf16[3,512,512]{2,1,0:T(8,128)(2,1)S(1)} %get-tuple-element.15.weight_ref, bf16[512,128]{1,0:T(8,128)(2,1)S(1)} %get-tuple-element.13.q_ref, ...), custom_call_target="tpu_custom_call" | custom-call | flops 469762048 | bytes 1048576 | tf_op jit(solution)/shard_map/far/pallas_call | solution.py:140
  25.6 8.9 %collective-permute-start.2 = (bf16[1024,128]{1,0:T(8,128)(2,1)S(1)}, bf16[1024,128]{1,0:T(8,128)(2,1)S(1)}, u32[]{:S(2)}, u32[]{:S(2)}) collective-permute-start(bf16[1024,128]{1,0:T(8,128)(2,1)S(1)} %get-tuple-element.19), channel_id=1, source_target_pairs={{2,0},{3,1},{4,2},{5,3},{6,4},{7,5},{8,6},{9,7},{10,8},{11,9},{12,... | collective-permute-start | bytes 786440 | tf_op jit(solution)/shard_map/ppermute | solution.py:21
  34.6 2.4 %collective-permute-start.3 = (bf16[1024,128]{1,0:T(8,128)(2,1)S(1)}, bf16[1024,128]{1,0:T(8,128)(2,1)S(1)}, u32[]{:S(2)}, u32[]{:S(2)}) collective-permute-start(bf16[1024,128]{1,0:T(8,128)(2,1)S(1)} %get-tuple-element.20), channel_id=1, source_target_pairs={{1,0},{2,1},{3,2},{4,3},{5,4},{6,5},{7,6},{8,7},{9,8},{10,9},{11,1... | collective-permute-start | bytes 786440 | tf_op jit(solution)/shard_map/ppermute | solution.py:21
  37.0 2.6 %own.1 = (bf16[512,128]{1,0:T(8,128)(2,1)}, f32[1024,128]{1,0:T(8,128)S(1)}) custom-call(s32[1]{0:T(128)} %bitcast.shard_ref, s32[1,512]{1,0:T(1,128)S(1)} %get-tuple-element.12.start_ref, f32[1,512]{1,0:T(1,128)S(1)} %get-tuple-element.14.lse_ref, f32[1,512]{1,0:T(1,128)S(1)} %get-tuple-element.16.delta_ref, bf16[512,128]{1,0:T(8,128)(2,1)S(1)} %get-tuple-element.13.q_ref, ...), custom_call_target="tpu_custom_call" | custom-call | flops 738197504 | bytes 1048576 | tf_op jit(solution)/shard_map/own/pallas_call | solution.py:140
  39.6 0.0 collective-permute-done.2.two_ref
  39.6 2.3 %collective-permute-done.3.one_ref = bf16[1024,128]{1,0:T(8,128)(2,1)S(1)} collective-permute-done((bf16[1024,128]{1,0:T(8,128)(2,1)S(1)}, bf16[1024,128]{1,0:T(8,128)(2,1)S(1)}, u32[]{:S(2)}, u32[]{:S(2)}) %collective-permute-start.3) | collective-permute-done | bytes 262176 | tf_op jit(solution)/shard_map/ppermute | solution.py:21
  41.9 0.1 total.1
  42.0 13.6 %all_to_all.10 = bf16[8,2,64,128]{3,2,1,0:T(8,128)(2,1)S(1)} all-to-all(bf16[8,2,64,128]{3,2,1,0:T(8,128)(2,1)S(1)} %total.1), channel_id=1, replica_groups=mesh['head'=8,'ctx'=64] {'head'}, dimensions={0} | all-to-all | bytes 524288 | tf_op jit(solution)/shard_map/all_to_all | solution.py:208
  55.7 0.6 %fusion = (bf16[1,64,128]{2,1,0:T(8,128)(2,1)}, bf16[1,64,128]{2,1,0:T(8,128)(2,1)}) fusion(bf16[2,64,128]{2,1,0:T(8,128)(2,1)S(1)} %reduce_sum.12), kind=kLoop, calls=%fused_computation.2 | loop fusion | bytes 65536 | tf_op jit(solution)/shard_map/slice | solution.py:210
  (1 shorter events, 0.0 us)
Async XLA Ops:
  0.6 7.3 %copy-start = (bf16[1,64,1024]{2,1,0:T(8,128)(2,1)S(1)}, bf16[1,64,1024]{2,1,0:T(8,128)(2,1)}, u32[]{:S(2)}) copy-start(bf16[1,64,1024]{2,1,0:T(8,128)(2,1)} %param.8) | copy-start | bytes 393220
  1.7 18.3 %collective-permute-start.1 = (bf16[1024,128]{1,0:T(8,128)(2,1)S(1)}, bf16[1024,128]{1,0:T(8,128)(2,1)S(1)}, u32[]{:S(2)}, u32[]{:S(2)}) collective-permute-start(bf16[1024,128]{1,0:T(8,128)(2,1)S(1)} %pad_add_fusion.kv0_ref), channel_id=1, source_target_pairs={{0,2},{1,3},{2,4},{3,5},{4,6},{5,7},{6,8},{7,9},{8,10},{9,11},{10,... | collective-permute-start | bytes 786440 | tf_op jit(solution)/shard_map/ppermute | solution.py:21
  6.0 16.0 %collective-permute-start = (bf16[1024,128]{1,0:T(8,128)(2,1)S(1)}, bf16[1024,128]{1,0:T(8,128)(2,1)S(1)}, u32[]{:S(2)}, u32[]{:S(2)}) collective-permute-start(bf16[1024,128]{1,0:T(8,128)(2,1)S(1)} %pad_add_fusion.kv0_ref), channel_id=1, source_target_pairs={{0,1},{1,2},{2,3},{3,4},{4,5},{5,6},{6,7},{7,8},{8,9},{9,10},{10,1... | collective-permute-start | bytes 786440 | tf_op jit(solution)/shard_map/ppermute | solution.py:21
  8.6 16.1 %all-to-all-start = ((bf16[8,64,128]{2,1,0:T(8,128)(2,1)}), bf16[8,64,128]{2,1,0:T(8,128)(2,1)S(1)}, u32[]{:S(2)}, u32[]{:S(2)}) async-start(bf16[8,64,128]{2,1,0:T(8,128)(2,1)} %copy_bitcast_fusion), calls=%async_computation | async-start | bytes 262144 | tf_op jit(solution)/shard_map/all_to_all | solution.py:168
  15.7 0.9 %copy-start.1 = (bf16[512,128]{1,0:T(8,128)(2,1)S(1)}, bf16[512,128]{1,0:T(8,128)(2,1)}, u32[]{:S(2)}) copy-start(bf16[512,128]{1,0:T(8,128)(2,1)} %q_ref.1) | copy-start | bytes 393220
  16.6 0.7 %copy-start.2 = (s32[64]{0:T(128)S(1)}, s32[64]{0:T(128)}, u32[]{:S(2)}) copy-start(s32[64]{0:T(128)} %param.9) | copy-start | bytes 772
  25.6 13.9 %collective-permute-start.2 = (bf16[1024,128]{1,0:T(8,128)(2,1)S(1)}, bf16[1024,128]{1,0:T(8,128)(2,1)S(1)}, u32[]{:S(2)}, u32[]{:S(2)}) collective-permute-start(bf16[1024,128]{1,0:T(8,128)(2,1)S(1)} %get-tuple-element.19), channel_id=1, source_target_pairs={{2,0},{3,1},{4,2},{5,3},{6,4},{7,5},{8,6},{9,7},{10,8},{11,9},{12,... | collective-permute-start | bytes 786440 | tf_op jit(solution)/shard_map/ppermute | solution.py:21
  34.6 7.3 %collective-permute-start.3 = (bf16[1024,128]{1,0:T(8,128)(2,1)S(1)}, bf16[1024,128]{1,0:T(8,128)(2,1)S(1)}, u32[]{:S(2)}, u32[]{:S(2)}) collective-permute-start(bf16[1024,128]{1,0:T(8,128)(2,1)S(1)} %get-tuple-element.20), channel_id=1, source_target_pairs={{1,0},{2,1},{3,2},{4,3},{5,4},{6,5},{7,6},{8,7},{9,8},{10,9},{11,1... | collective-permute-start | bytes 786440 | tf_op jit(solution)/shard_map/ppermute | solution.py:21
